TPU v7x, 32 devices: a whole 2x2x4 slice. The times are simulated.
32 devices in a mesh: row: 8 (over z, x), rep: 4 (over y, core).
Axes of the slice: x: 2, y: 2, z: 4, core: 2. Of those that a mesh axis runs over, the one named last changes fastest.
Arguments:
- features: bfloat16 [8192, 256], P('row'), may hold values from -6 to 6
- block_cols: int32 [64, 4, 12], P('row', 'rep'), may hold values from 0 to 63, as said below
- block_vals: bfloat16 [64, 4, 12, 128, 128], P('row', 'rep'), may hold values from -0.078125 to 0.078125
- weight: bfloat16 [256, 256], replicated, may hold values from -0.375 to 0.375
- cotangent: bfloat16 [8192, 256], P(('row', 'rep')), may hold values from -6 to 6
Outputs:
- output_rows: bfloat16 [8192, 256], P(('row', 'rep'))
- grad_weight: float32 [256, 256], replicated
- grad_features: float32 [8192, 256], P(('row', 'rep'))
Inputs may be any that keep to these rules, and one draw needn't show every extreme that they name: For a node block b of row group g = b // 8 and quarter index r, every entry block_cols[b, r, s] equals h * 8 + r * 2 + q with h a row group within 3 of g (and inside the grid) and 0 <= q < 2; entries may repeat.
All inputs are finite; a program needn't handle non-finite values.
Results may differ from a plain program's by a relative error of at most 0.0065.
Values may be sent and summed in bfloat16 or wider, within the bound.
A program may use at most 64 MiB of HBM per device.

v0:
```python
import jax
import jax.numpy as jnp
from jax import lax
from jax.sharding import PartitionSpec as P

HALF = 3


def from_behind(x, axis, by):
    devices = lax.axis_size(axis)
    pairs = [(i, i + by) for i in range(devices) if 0 <= i + by < devices]
    return lax.ppermute(x, axis, pairs)


def gather_band(own_quarter):
    sections = 2 * HALF + 1
    pieces = []
    for section in range(sections):
        if section == HALF:
            pieces.append(own_quarter)
        else:
            pieces.append(from_behind(own_quarter, "row", section - HALF))
    return jnp.stack(pieces)


def return_band(window_grad):
    sections = 2 * HALF + 1
    accumulated = window_grad[HALF]
    for section in range(sections):
        if section != HALF:
            accumulated = accumulated + from_behind(window_grad[section], "row", HALF - section)
    return accumulated


def on_device(features, block_cols, block_vals, weight, cotangent):
    rep_count = lax.axis_size("rep")
    row_count = lax.axis_size("row")
    rep_index = lax.axis_index("rep")
    row_index = lax.axis_index("row")
    group_rows, hidden = features.shape
    block_side = block_vals.shape[-1]
    blocks_group = group_rows // block_side
    quarter_blocks = blocks_group // rep_count
    sections = 2 * HALF + 1
    own_quarter = lax.dynamic_slice_in_dim(
        features, rep_index * quarter_blocks * block_side, quarter_blocks * block_side, 0
    )
    own_quarter = own_quarter.reshape(quarter_blocks, block_side, hidden)
    window = gather_band(own_quarter)
    window_rows = window.reshape(sections * quarter_blocks, block_side, hidden)
    column_ids = block_cols[:, 0, :]
    block_values = block_vals[:, 0]
    source_group = column_ids // blocks_group
    within = column_ids % blocks_group - rep_index * quarter_blocks
    slot_index = (row_index + HALF - source_group) * quarter_blocks + within
    chosen = window_rows[slot_index]
    partial_rows = jnp.einsum(
        "bsij,bsjh->bih", block_values, chosen, preferred_element_type=jnp.float32
    )
    partial_rows = partial_rows.reshape(group_rows, hidden)
    summed = lax.psum_scatter(partial_rows, "rep", scatter_dimension=0, tiled=True)
    aggregate = summed.astype(jnp.bfloat16)
    preact = jnp.dot(aggregate, weight, preferred_element_type=jnp.float32)
    output_rows = jax.nn.silu(preact).astype(jnp.bfloat16)
    sigmoid_pre = jax.nn.sigmoid(preact)
    grad_pre = (
        cotangent.astype(jnp.float32) * sigmoid_pre * (1.0 + preact * (1.0 - sigmoid_pre))
    ).astype(jnp.bfloat16)
    local_grad = lax.dot_general(
        aggregate, grad_pre, (((0,), (0,)), ((), ())), preferred_element_type=jnp.float32
    )
    node_count = group_rows * row_count
    grad_weight = lax.psum(local_grad, ("row", "rep")) * node_count ** (-0.5)
    backward = lax.dot_general(
        grad_pre, weight, (((1,), (1,)), ((), ())), preferred_element_type=jnp.float32
    )
    backward = backward.astype(jnp.bfloat16)
    back_group = lax.all_gather(backward, "rep", axis=0, tiled=True).reshape(
        blocks_group, block_side, hidden
    )
    selector = (
        slot_index[:, :, None] == jnp.arange(sections * quarter_blocks)[None, None, :]
    ).astype(jnp.bfloat16)
    per_slot = jnp.einsum(
        "bsc,bsji->cbji", selector, block_values, preferred_element_type=jnp.float32
    )
    upper_part = per_slot.astype(jnp.bfloat16)
    lower_part = (per_slot - upper_part.astype(jnp.float32)).astype(jnp.bfloat16)
    window_grad = jnp.einsum(
        "cbji,bjh->cih", upper_part, back_group, preferred_element_type=jnp.float32
    )
    window_grad = window_grad + jnp.einsum(
        "cbji,bjh->cih", lower_part, back_group, preferred_element_type=jnp.float32
    )
    window_grad = window_grad.reshape(sections, quarter_blocks, block_side, hidden)
    grad_features = return_band(window_grad).reshape(quarter_blocks * block_side, hidden)
    return (output_rows, grad_weight, grad_features)


def solution(mesh):
    return jax.shard_map(
        on_device,
        mesh=mesh,
        in_specs=(
            P("row", None),
            P("row", "rep", None),
            P("row", "rep", None, None, None),
            P(),
            P(("row", "rep"), None),
        ),
        out_specs=(P(("row", "rep"), None), P(), P(("row", "rep"), None)),
        check_vma=False,
    )
```

profile of v0, /device:TPU:10, one launch (start us, length us, event | category | flops | bytes accessed | tf_op | source)
XLA Modules:
  0.0 249.4 jit_solution(16847574456233830275)
XLA Ops:
  7.2 1.1 constant_dynamic-slice_fusion
  8.3 4.5 %collective-permute-start.5 = (bf16[2,128,256]{2,1,0:T(8,128)(2,1)S(1)}, bf16[2,128,256]{2,1,0:T(8,128)(2,1)S(1)}, u32[]{:S(2)}, u32[]{:S(2)}) collective-permute-start(bf16[2,128,256]{2,1,0:T(8,128)(2,1)S(1)} %bitcast.67), channel_id=1, source_target_pairs={{0,12},{4,16},{8,20},{12,24},{16,28},{1,13},{5,17},{9,21},{13,25},... | collective-permute-start | bytes 393224 | tf_op jit(solution)/shard_map/ppermute | solution.py:12
  12.8 1.9 collective-permute-start.4
  14.7 3.4 %collective-permute-start.3 = (bf16[2,128,256]{2,1,0:T(8,128)(2,1)S(1)}, bf16[2,128,256]{2,1,0:T(8,128)(2,1)}, u32[]{:S(2)}, u32[]{:S(2)}) collective-permute-start(bf16[2,128,256]{2,1,0:T(8,128)(2,1)S(1)} %bitcast.69), channel_id=1, source_target_pairs={{0,4},{4,8},{8,12},{12,16},{16,20},{20,24},{24,28},{1,5},{5,9},{9,... | collective-permute-start | bytes 393224 | tf_op jit(solution)/shard_map/ppermute | solution.py:12
  18.1 2.5 collective-permute-start.2
  20.6 3.3 %collective-permute-start = (bf16[2,128,256]{2,1,0:T(8,128)(2,1)S(1)}, bf16[2,128,256]{2,1,0:T(8,128)(2,1)}, u32[]{:S(2)}, u32[]{:S(2)}) collective-permute-start(bf16[2,128,256]{2,1,0:T(8,128)(2,1)S(1)} %bitcast.71), channel_id=1, source_target_pairs={{12,0},{16,4},{20,8},{24,12},{28,16},{13,1},{17,5},{21,9},{25,13},... | collective-permute-start | bytes 393224 | tf_op jit(solution)/shard_map/ppermute | solution.py:12
  24.7 4.7 %collective-permute-done = bf16[2,128,256]{2,1,0:T(8,128)(2,1)} collective-permute-done((bf16[2,128,256]{2,1,0:T(8,128)(2,1)S(1)}, bf16[2,128,256]{2,1,0:T(8,128)(2,1)}, u32[]{:S(2)}, u32[]{:S(2)}) %collective-permute-start) | collective-permute-done | bytes 131104 | tf_op jit(solution)/shard_map/ppermute | solution.py:12
  29.5 5.5 %collective-permute-start.1 = (bf16[2,128,256]{2,1,0:T(8,128)(2,1)S(1)}, bf16[2,128,256]{2,1,0:T(8,128)(2,1)S(1)}, u32[]{:S(2)}, u32[]{:S(2)}) collective-permute-start(bf16[2,128,256]{2,1,0:T(8,128)(2,1)S(1)} %bitcast.72), channel_id=1, source_target_pairs={{8,0},{12,4},{16,8},{20,12},{24,16},{28,20},{9,1},{13,5},{17,9},{2... | collective-permute-start | bytes 393224 | tf_op jit(solution)/shard_map/ppermute | solution.py:12
  35.0 1.6 bitcast_dynamic-update-slice_fusion.5
  36.5 0.9 collective-permute-done.1
  38.1 1.6 bitcast_dynamic-update-slice_fusion.3
  40.4 1.6 bitcast_dynamic-update-slice_fusion.2
  43.2 7.2 %gather_fusion = bf16[96,128,256]{2,1,0:T(8,128)(2,1)} fusion(bf16[14,128,256]{2,1,0:T(8,128)(2,1)} %bitcast.8, s32[1024]{0:T(1024)S(1)} %pad_clamp_fusion), kind=kCustom, calls=%fused_computation | custom fusion | bytes 12583296 | tf_op jit(solution)/shard_map/gather | solution.py:56
  50.4 5.0 %fusion.36 = f32[8,256,128,1]{1,2,3,0:T(8,128)} fusion(bf16[8,12,128,256]{3,2,1,0:T(8,128)(2,1)} %bitcast.63, bf16[8,1,12,128,128]{4,3,2,1,0:T(8,128)(2,1)S(1)} %copy-done), kind=kOutput, calls=%fused_computation.65 | convolution fusion | flops 805306368 | bytes 10485760 | tf_op jit(solution)/shard_map/bsij,bsjh->bih/dot_general | solution.py:57
  55.5 5.2 %fusion.2 = f32[8,14,128,128]{3,1,2,0:T(8,128)} fusion(bf16[8,12,128,128]{3,2,1,0:T(8,128)(2,1)S(1)} %bitcast.62, s32[8,12]{1,0:T(8,128)S(1)} %fusion.26), kind=kOutput, calls=%fused_computation.5 | convolution fusion | flops 44041536 | bytes 10486144 | tf_op jit(solution)/shard_map/bsc,bsji->cbji/dot_general | solution.py:84
  60.8 19.8 %reduce-scatter.2.cloned.1.call-done = f32[256,256]{1,0:T(8,128)} async-done(((f32[1024,256]{1,0:T(8,128)}), f32[256,256]{1,0:T(8,128)}) %reduce-scatter.2.cloned.1.call-update) | async-done | bytes 262160 | tf_op jit(solution)/shard_map/reduce_scatter | solution.py:61
  80.5 2.0 multiply_convert_fusion
  82.8 7.1 %all_gather.3 = bf16[1024,256]{1,0:T(8,128)(2,1)S(1)} all-gather(bf16[256,256]{1,0:T(8,128)(2,1)S(1)} %convolution_convert_fusion), channel_id=1, replica_groups=mesh['row'=8,'rep'=4] {'rep'}, dimensions={0}, use_global_device_ids=true | all-gather | bytes 655360 | tf_op jit(solution)/shard_map/all_gather | solution.py:78
  89.9 7.2 %fusion.1 = f32[14,128,256,1]{2,1,3,0:T(8,128)S(1)} fusion(bf16[8,128,256,1]{2,1,0,3:T(8,128)(2,1)S(1)} %bitcast.65, f32[8,14,128,128]{3,1,2,0:T(8,128)} %fusion.2), kind=kOutput, calls=%fused_computation.4 | convolution fusion | flops 939524096 | bytes 9699328 | tf_op jit(solution)/shard_map/cbji,bjh->cih/dot_general | solution.py:89
  97.1 3.9 %bitcast_add_fusion = f32[14,128,256]{2,1,0:T(8,128)S(1)} fusion(f32[14,128,256,1]{2,1,3,0:T(8,128)S(1)} %fusion.1, bf16[8,128,256,1]{2,1,0,3:T(8,128)(2,1)S(1)} %bitcast.66, f32[8,14,128,128]{3,1,2,0:T(8,128)S(1)} %copy-done.1), kind=kOutput, calls=%fused_computation.8 | convolution fusion | flops 947322880 | bytes 11534336 | tf_op jit(solution)/shard_map/cbji,bjh->cih/dot_general | solution.py:92
  101.1 1.3 copy-done.2
  102.3 1.1 fusion.38
  103.4 4.3 %collective-permute-start.6 = (f32[2,128,256]{2,1,0:T(8,128)}, f32[2,128,256]{2,1,0:T(8,128)}, u32[]{:S(2)}, u32[]{:S(2)}) collective-permute-start(f32[2,128,256]{2,1,0:T(8,128)} %get-tuple-element.3), channel_id=1, source_target_pairs={{0,12},{4,16},{8,20},{12,24},{16,28},{1,13},{5,17},{9,21},{13,25},... | collective-permute-start | bytes 786440 | tf_op jit(solution)/shard_map/ppermute | solution.py:12
  107.7 0.9 fusion.13
  108.6 3.1 %collective-permute-start.11 = (f32[2,128,256]{2,1,0:T(8,128)}, f32[2,128,256]{2,1,0:T(8,128)}, u32[]{:S(2)}, u32[]{:S(2)}) collective-permute-start(f32[2,128,256]{2,1,0:T(8,128)} %get-tuple-element.4), channel_id=1, source_target_pairs={{12,0},{16,4},{20,8},{24,12},{28,16},{13,1},{17,5},{21,9},{25,13},... | collective-permute-start | bytes 786440 | tf_op jit(solution)/shard_map/ppermute | solution.py:12
  111.8 1.9 collective-permute-start.10
  113.7 1.9 collective-permute-start.9
  115.6 4.8 %collective-permute-start.8 = (f32[2,128,256]{2,1,0:T(8,128)}, f32[2,128,256]{2,1,0:T(8,128)}, u32[]{:S(2)}, u32[]{:S(2)}) collective-permute-start(f32[2,128,256]{2,1,0:T(8,128)} %get-tuple-element.7), channel_id=1, source_target_pairs={{0,4},{4,8},{8,12},{12,16},{16,20},{20,24},{24,28},{1,5},{5,9},{9,... | collective-permute-start | bytes 786440 | tf_op jit(solution)/shard_map/ppermute | solution.py:12
  120.5 4.1 %collective-permute-start.7 = (f32[2,128,256]{2,1,0:T(8,128)S(1)}, f32[2,128,256]{2,1,0:T(8,128)}, u32[]{:S(2)}, u32[]{:S(2)}) collective-permute-start(f32[2,128,256]{2,1,0:T(8,128)S(1)} %get-tuple-element.8), channel_id=1, source_target_pairs={{0,8},{4,12},{8,16},{12,20},{16,24},{20,28},{1,9},{5,13},{9,17},{1... | collective-permute-start | bytes 786440 | tf_op jit(solution)/shard_map/ppermute | solution.py:12
  124.6 114.0 %all-reduce.2.cloned.1.call-done = f32[256,256]{1,0:T(8,128)} async-done(((f32[256,256]{1,0:T(8,128)}), f32[256,256]{1,0:T(8,128)}) %all-reduce.2.cloned.1.call-update) | async-done | bytes 262160 | tf_op jit(solution)/shard_map/psum | solution.py:73
  238.6 1.7 broadcast_multiply_fusion
  240.3 2.2 fusion.12
  (36 shorter events, 3.8 us)
Async XLA Ops:
  7.2 43.2 %copy-start = (bf16[8,1,12,128,128]{4,3,2,1,0:T(8,128)(2,1)S(1)}, bf16[8,1,12,128,128]{4,3,2,1,0:T(8,128)(2,1)}, u32[]{:S(2)}) copy-start(bf16[8,1,12,128,128]{4,3,2,1,0:T(8,128)(2,1)} %param.7) | copy-start | bytes 9437188
  7.2 73.3 %reduce-scatter.2.cloned.1.call-start = ((), (), s32[]{:S(2)}) async-start(), calls=%async_computation.1 | async-start | bytes 1310720 | tf_op jit(solution)/shard_map/reduce_scatter | solution.py:61
  8.3 34.3 %collective-permute-start.5 = (bf16[2,128,256]{2,1,0:T(8,128)(2,1)S(1)}, bf16[2,128,256]{2,1,0:T(8,128)(2,1)S(1)}, u32[]{:S(2)}, u32[]{:S(2)}) collective-permute-start(bf16[2,128,256]{2,1,0:T(8,128)(2,1)S(1)} %bitcast.67), channel_id=1, source_target_pairs={{0,12},{4,16},{8,20},{12,24},{16,28},{1,13},{5,17},{9,21},{13,25},... | collective-permute-start | bytes 393224 | tf_op jit(solution)/shard_map/ppermute | solution.py:12
  12.8 29.1 %collective-permute-start.4 = (bf16[2,128,256]{2,1,0:T(8,128)(2,1)S(1)}, bf16[2,128,256]{2,1,0:T(8,128)(2,1)S(1)}, u32[]{:S(2)}, u32[]{:S(2)}) collective-permute-start(bf16[2,128,256]{2,1,0:T(8,128)(2,1)S(1)} %bitcast.68), channel_id=1, source_target_pairs={{0,8},{4,12},{8,16},{12,20},{16,24},{20,28},{1,9},{5,13},{9,17},{1... | collective-permute-start | bytes 393224 | tf_op jit(solution)/shard_map/ppermute | solution.py:12
  14.7 25.7 %collective-permute-start.3 = (bf16[2,128,256]{2,1,0:T(8,128)(2,1)S(1)}, bf16[2,128,256]{2,1,0:T(8,128)(2,1)}, u32[]{:S(2)}, u32[]{:S(2)}) collective-permute-start(bf16[2,128,256]{2,1,0:T(8,128)(2,1)S(1)} %bitcast.69), channel_id=1, source_target_pairs={{0,4},{4,8},{8,12},{12,16},{16,20},{20,24},{24,28},{1,5},{5,9},{9,... | collective-permute-start | bytes 393224 | tf_op jit(solution)/shard_map/ppermute | solution.py:12
  18.1 20.0 %collective-permute-start.2 = (bf16[2,128,256]{2,1,0:T(8,128)(2,1)S(1)}, bf16[2,128,256]{2,1,0:T(8,128)(2,1)}, u32[]{:S(2)}, u32[]{:S(2)}) collective-permute-start(bf16[2,128,256]{2,1,0:T(8,128)(2,1)S(1)} %bitcast.70), channel_id=1, source_target_pairs={{4,0},{8,4},{12,8},{16,12},{20,16},{24,20},{28,24},{5,1},{9,5},{13... | collective-permute-start | bytes 393224 | tf_op jit(solution)/shard_map/ppermute | solution.py:12
  20.6 8.9 %collective-permute-start = (bf16[2,128,256]{2,1,0:T(8,128)(2,1)S(1)}, bf16[2,128,256]{2,1,0:T(8,128)(2,1)}, u32[]{:S(2)}, u32[]{:S(2)}) collective-permute-start(bf16[2,128,256]{2,1,0:T(8,128)(2,1)S(1)} %bitcast.71), channel_id=1, source_target_pairs={{12,0},{16,4},{20,8},{24,12},{28,16},{13,1},{17,5},{21,9},{25,13},... | collective-permute-start | bytes 393224 | tf_op jit(solution)/shard_map/ppermute | solution.py:12
  29.5 8.0 %collective-permute-start.1 = (bf16[2,128,256]{2,1,0:T(8,128)(2,1)S(1)}, bf16[2,128,256]{2,1,0:T(8,128)(2,1)S(1)}, u32[]{:S(2)}, u32[]{:S(2)}) collective-permute-start(bf16[2,128,256]{2,1,0:T(8,128)(2,1)S(1)} %bitcast.72), channel_id=1, source_target_pairs={{8,0},{12,4},{16,8},{20,12},{24,16},{28,20},{9,1},{13,5},{17,9},{2... | collective-permute-start | bytes 393224 | tf_op jit(solution)/shard_map/ppermute | solution.py:12
  50.4 5.0 %copy-start.5 = (s32[8,1,12]{2,1,0:T(1,128)S(1)}, s32[8,1,12]{2,1,0:T(1,128)}, u32[]{:S(2)}) copy-start(s32[8,1,12]{2,1,0:T(1,128)} %param.6) | copy-start | bytes 1156
  55.4 183.2 %all-reduce.2.cloned.1.call-start = ((), (), s32[]{:S(2)}) async-start(), calls=%async_computation.2 | async-start | bytes 524288 | tf_op jit(solution)/shard_map/psum | solution.py:73
  55.5 25.1 %copy-start.4 = (bf16[256,256]{1,0:T(8,128)(2,1)S(1)}, bf16[256,256]{1,0:T(8,128)(2,1)}, u32[]{:S(2)}) copy-start(bf16[256,256]{1,0:T(8,128)(2,1)} %param.8) | copy-start | bytes 393220
  55.5 25.0 %copy-start.6 = (bf16[256,256]{1,0:T(8,128)(2,1)S(1)}, bf16[256,256]{1,0:T(8,128)(2,1)}, u32[]{:S(2)}) copy-start(bf16[256,256]{1,0:T(8,128)(2,1)} %param.9) | copy-start | bytes 393220
  80.5 16.6 %copy-start.1 = (f32[8,14,128,128]{3,1,2,0:T(8,128)S(1)}, f32[8,14,128,128]{3,1,2,0:T(8,128)}, u32[]{:S(2)}) copy-start(f32[8,14,128,128]{3,1,2,0:T(8,128)} %fusion.2) | copy-start | bytes 22020100
  97.1 10.6 %copy-start.3 = (f32[256,256]{1,0:T(8,128)S(1)}, f32[256,256]{1,0:T(8,128)}, u32[]{:S(2)}) copy-start(f32[256,256]{1,0:T(8,128)} %reduce-scatter.2.cloned.1.call-done) | copy-start | bytes 786436
  101.1 1.3 copy-start.2
  103.4 17.1 %collective-permute-start.6 = (f32[2,128,256]{2,1,0:T(8,128)}, f32[2,128,256]{2,1,0:T(8,128)}, u32[]{:S(2)}, u32[]{:S(2)}) collective-permute-start(f32[2,128,256]{2,1,0:T(8,128)} %get-tuple-element.3), channel_id=1, source_target_pairs={{0,12},{4,16},{8,20},{12,24},{16,28},{1,13},{5,17},{9,21},{13,25},... | collective-permute-start | bytes 786440 | tf_op jit(solution)/shard_map/ppermute | solution.py:12
  108.6 131.6 %collective-permute-start.11 = (f32[2,128,256]{2,1,0:T(8,128)}, f32[2,128,256]{2,1,0:T(8,128)}, u32[]{:S(2)}, u32[]{:S(2)}) collective-permute-start(f32[2,128,256]{2,1,0:T(8,128)} %get-tuple-element.4), channel_id=1, source_target_pairs={{12,0},{16,4},{20,8},{24,12},{28,16},{13,1},{17,5},{21,9},{25,13},... | collective-permute-start | bytes 786440 | tf_op jit(solution)/shard_map/ppermute | solution.py:12
  111.8 128.5 %collective-permute-start.10 = (f32[2,128,256]{2,1,0:T(8,128)}, f32[2,128,256]{2,1,0:T(8,128)}, u32[]{:S(2)}, u32[]{:S(2)}) collective-permute-start(f32[2,128,256]{2,1,0:T(8,128)} %get-tuple-element.5), channel_id=1, source_target_pairs={{8,0},{12,4},{16,8},{20,12},{24,16},{28,20},{9,1},{13,5},{17,9},{2... | collective-permute-start | bytes 786440 | tf_op jit(solution)/shard_map/ppermute | solution.py:12
  113.7 126.5 %collective-permute-start.9 = (f32[2,128,256]{2,1,0:T(8,128)}, f32[2,128,256]{2,1,0:T(8,128)}, u32[]{:S(2)}, u32[]{:S(2)}) collective-permute-start(f32[2,128,256]{2,1,0:T(8,128)} %get-tuple-element.6), channel_id=1, source_target_pairs={{4,0},{8,4},{12,8},{16,12},{20,16},{24,20},{28,24},{5,1},{9,5},{13... | collective-permute-start | bytes 786440 | tf_op jit(solution)/shard_map/ppermute | solution.py:12
  115.6 124.6 %collective-permute-start.8 = (f32[2,128,256]{2,1,0:T(8,128)}, f32[2,128,256]{2,1,0:T(8,128)}, u32[]{:S(2)}, u32[]{:S(2)}) collective-permute-start(f32[2,128,256]{2,1,0:T(8,128)} %get-tuple-element.7), channel_id=1, source_target_pairs={{0,4},{4,8},{8,12},{12,16},{16,20},{20,24},{24,28},{1,5},{5,9},{9,... | collective-permute-start | bytes 786440 | tf_op jit(solution)/shard_map/ppermute | solution.py:12
  120.5 119.8 %collective-permute-start.7 = (f32[2,128,256]{2,1,0:T(8,128)S(1)}, f32[2,128,256]{2,1,0:T(8,128)}, u32[]{:S(2)}, u32[]{:S(2)}) collective-permute-start(f32[2,128,256]{2,1,0:T(8,128)S(1)} %get-tuple-element.8), channel_id=1, source_target_pairs={{0,8},{4,12},{8,16},{12,20},{16,24},{20,28},{1,9},{5,13},{9,17},{1... | collective-permute-start | bytes 786440 | tf_op jit(solution)/shard_map/ppermute | solution.py:12
Sparse Core Ops, SparseCore 0:
  55.5 24.9 reduce-scatter.1
  108.8 129.7 all-reduce.1
where the time goes:
time: 252 us; the launch traced here: 249 us
  waiting for transfers between devices  139 us (55%)
  starting transfers between devices  41.3 us (16%)
  matrix products  24.5 us (10%)
  local copies, waits for them, and re-layouts  18 us (7%)
  between operations  14.3 us (6%)
  blocking collectives  7.1 us (3%)
  other arithmetic  4.65 us (2%)
    psum x1, waiting for transfers between devices, on_device(): grad_weight = lax.psum(local_grad, ('row', 'rep')) * node_count ** (-0.5)  114 us
    ppermute x12, starting transfers between devices, from_behind(): return lax.ppermute(x, axis, pairs)  41.3 us
    reduce_scatter x1, waiting for transfers between devices, on_device(): lax.psum_scatter(partial_rows, 'rep', scatter_dimension=0, tiled=True)  19.8 us
    unnamed x20, local copies, waits for them, and re-layouts  7.96 us
    dot_general x1, matrix products, on_device(): jnp.einsum('cbji,bjh->cih', upper_part, back_group, preferred_element_typ...  7.18 us
    gather x1, local copies, waits for them, and re-layouts, on_device(): chosen = window_rows[slot_index]  7.16 us
    all_gather x1, blocking collectives, on_device(): lax.all_gather(backward, 'rep', axis=0, tiled=True)  7.1 us
    ppermute x12, waiting for transfers between devices, from_behind(): return lax.ppermute(x, axis, pairs)  5.68 us
  transfers between devices with their start and end apart: 14, of which 4 were waited for; matrix products, arithmetic and copies ran while one was open for 6% of the time, Pallas kernels for 0%

commit v1 on v0

v1 whole, which is shorter than its diff:
```python
import functools

import jax
import jax.numpy as jnp
from jax import lax
from jax.experimental import pallas as pl
from jax.experimental.pallas import tpu as pltpu
from jax.sharding import PartitionSpec as P

HALF = 3
SECTIONS = 2 * HALF + 1


def flip(index, bit):
    return index + bit * (1 - 2 * ((index // bit) % 2))


def flip_all(index, mask):
    bit = 1
    while bit <= mask:
        if mask & bit:
            index = flip(index, bit)
        bit *= 2
    return index


def remote(src, dst, send_sem, recv_sem, device):
    return pltpu.make_async_remote_copy(
        src_ref=src,
        dst_ref=dst,
        send_sem=send_sem,
        recv_sem=recv_sem,
        device_id=device,
        device_id_type=pl.DeviceIdType.MESH,
    )


def layer_kernel(
    sizes,
    plan_ref, features_ref, vals_ref, weight_ref, cotangent_ref,
    out_ref, grad_weight_ref, grad_features_ref,
    vals, window, part_send, part_recv, back, run, back_send, back_recv,
    gw_send, gw_recv, bf_send, bf_recv, gw_all,
    local_sem, a_send, a_recv, b_send, b_recv, c_send, c_recv,
    d_send, d_recv, e_send, e_recv, f_send, f_recv, g_send, g_recv,
):
    rows, reps, quart, slots, blk, blocks = sizes
    pairs = blocks * slots
    row = lax.axis_index("row")
    rep = lax.axis_index("rep")
    bits = [1 << k for k in range(rows.bit_length() - 1)]
    offsets = [d for d in (3, -3, 2, -2, 1, -1)]
    masks = sorted(range(1, reps), key=lambda m: -m)

    def inside(d):
        return jnp.logical_and(row + d >= 0, row + d < rows)

    vals_copy = pltpu.make_async_copy(vals_ref, vals, local_sem.at[0])
    vals_copy.start()
    own = features_ref.at[pl.ds(rep * quart, quart)]
    own_copy = pltpu.make_async_copy(own, window.at[pl.ds(HALF * quart, quart)], local_sem.at[1])
    own_copy.start()

    barrier = pltpu.get_barrier_semaphore()
    expected = reps - 1
    for d in offsets:
        @pl.when(inside(d))
        def _():
            pl.semaphore_signal(
                barrier, inc=1, device_id=(row + d, rep), device_id_type=pl.DeviceIdType.MESH
            )
        expected = expected + inside(d).astype(jnp.int32)
    for bit in bits:
        if bit > 2:
            pl.semaphore_signal(
                barrier, inc=1, device_id=(flip(row, bit), rep),
                device_id_type=pl.DeviceIdType.MESH,
            )
            expected = expected + 1
    for mask in masks:
        pl.semaphore_signal(
            barrier, inc=1, device_id=(row, flip_all(rep, mask)),
            device_id_type=pl.DeviceIdType.MESH,
        )
    pl.semaphore_wait(barrier, expected)

    def section(ref, j):
        return ref.at[pl.ds(j * quart, quart)]

    def feature_copy(d):
        return remote(
            own, section(window, HALF - d), a_send.at[HALF - d], a_recv.at[HALF - d],
            (row + d, rep),
        )

    for d in offsets:
        @pl.when(inside(d))
        def _():
            feature_copy(d).start()

        @pl.when(jnp.logical_not(inside(d)))
        def _():
            for q in range(quart):
                window[(HALF + d) * quart + q] = jnp.zeros(window.shape[1:], window.dtype)
                back_recv[(HALF + d) * quart + q] = jnp.zeros(
                    back_recv.shape[1:], back_recv.dtype
                )
    vals_copy.wait()
    own_copy.wait()
    for d in offsets:
        @pl.when(inside(d))
        def _():
            remote(
                own, section(window, HALF + d), a_send.at[HALF + d], a_recv.at[HALF + d],
                (row + d, rep),
            ).wait_recv()

    def partial(b):
        total = None
        for s in range(0, slots, 2):
            left = jnp.concatenate([vals[b * slots + s], vals[b * slots + s + 1]], axis=1)
            right = jnp.concatenate(
                [window[plan_ref[b * slots + s]], window[plan_ref[b * slots + s + 1]]], axis=0
            )
            term = jnp.dot(left, right, preferred_element_type=jnp.float32)
            total = term if total is None else total + term
        return total

    def part_copy(mask):
        return remote(
            part_send.at[mask - 1], part_recv.at[mask - 1], b_send.at[mask - 1],
            b_recv.at[mask - 1], (row, flip_all(rep, mask)),
        )

    for mask in masks:
        target = flip_all(rep, mask)
        for q in range(quart):
            part_send[mask - 1, q * blk:(q + 1) * blk] = partial(target * quart + q).astype(
                jnp.bfloat16
            )
        part_copy(mask).start()
    total = jnp.concatenate([partial(rep * quart + q) for q in range(quart)], axis=0)
    for mask in reversed(masks):
        part_copy(mask).wait_recv()
        total = total + part_recv[mask - 1].astype(jnp.float32)

    aggregate = total.astype(jnp.bfloat16)
    weight = weight_ref[...]
    preact = jnp.dot(aggregate, weight, preferred_element_type=jnp.float32)
    sigmoid_pre = jax.nn.sigmoid(preact)
    grad_pre = (
        cotangent_ref[...].astype(jnp.float32)
        * sigmoid_pre
        * (1.0 + preact * (1.0 - sigmoid_pre))
    ).astype(jnp.bfloat16)
    back_t = lax.dot_general(
        weight, grad_pre, (((1,), (1,)), ((), ())), preferred_element_type=jnp.float32
    ).astype(jnp.bfloat16)
    for q in range(quart):
        back[rep * quart + q] = back_t[:, q * blk:(q + 1) * blk]

    def back_copy(mask, owner):
        spot = section(back, owner)
        return remote(
            spot, spot, c_send.at[mask - 1], c_recv.at[mask - 1], (row, flip_all(rep, mask))
        )

    for mask in masks:
        back_copy(mask, rep).start()
    out_ref[...] = (preact * sigmoid_pre).astype(jnp.bfloat16)

    gw_send[...] = lax.dot_general(
        aggregate, grad_pre, (((0,), (0,)), ((), ())), preferred_element_type=jnp.float32
    )
    share = gw_send.shape[0] // reps

    def share_of(ref, owner):
        return ref.at[pl.ds(owner * share, share)]

    def scatter_copy(mask):
        target = flip_all(rep, mask)
        return remote(
            share_of(gw_send, target), gw_recv.at[mask - 1], e_send.at[mask - 1],
            e_recv.at[mask - 1], (row, target),
        )

    def row_copy(k):
        return remote(
            bf_send.at[k], bf_recv.at[k], f_send.at[k], f_recv.at[k], (flip(row, bits[k]), rep)
        )

    def gather_copy(mask, owner):
        spot = share_of(gw_all, owner)
        return remote(
            spot, spot, g_send.at[mask - 1], g_recv.at[mask - 1], (row, flip_all(rep, mask))
        )

    for mask in masks:
        scatter_copy(mask).start()
    for mask in reversed(masks):
        back_copy(mask, flip_all(rep, mask)).wait_recv()

    def backward(start, stop, acc):
        def step(k, acc):
            pair = plan_ref[pairs + k]
            block = plan_ref[2 * pairs + k]
            keep = plan_ref[3 * pairs + k]
            term = jnp.dot(back[block], vals[pair], preferred_element_type=jnp.float32)
            acc = jnp.where(keep > 0, acc, 0.0) + term
            run[k] = acc
            return acc
        return lax.fori_loop(start, stop, step, acc, unroll=8)

    acc = jnp.zeros(run.shape[1:], jnp.float32)
    acc = backward(0, pairs // 3, acc)
    mine = gw_send[pl.ds(rep * share, share)]
    for mask in reversed(masks):
        scatter_copy(mask).wait_recv()
        mine = mine + gw_recv[mask - 1]
    bf_send[0] = mine
    row_copy(0).start()
    acc = backward(pairs // 3, 2 * pairs // 3, acc)
    row_copy(0).wait_recv()
    bf_send[1] = bf_send[0] + bf_recv[0]
    row_copy(1).start()
    acc = backward(2 * pairs // 3, pairs, acc)

    def section_sum(j, q):
        c = j * quart + q
        last = plan_ref[4 * pairs + c]
        some = plan_ref[4 * pairs + SECTIONS * quart + c]
        return jnp.where(some > 0, run[last], 0.0)

    def grad_copy(d):
        return remote(
            section(back_send, HALF + d), section(back_recv, HALF - d), d_send.at[HALF - d],
            d_recv.at[HALF - d], (row + d, rep),
        )

    for d in offsets:
        for q in range(quart):
            back_send[(HALF + d) * quart + q] = section_sum(HALF + d, q).astype(jnp.bfloat16)

        @pl.when(inside(d))
        def _():
            grad_copy(d).start()

    for k in range(1, len(bits)):
        row_copy(k).wait_recv()
        summed = bf_send[k] + bf_recv[k]
        if k + 1 < len(bits):
            bf_send[k + 1] = summed
            row_copy(k + 1).start()
    gw_all[pl.ds(rep * share, share)] = summed
    for mask in masks:
        gather_copy(mask, rep).start()

    for d in reversed(offsets):
        @pl.when(inside(d))
        def _():
            remote(
                section(back_send, HALF + d), section(back_recv, HALF + d), d_send.at[HALF + d],
                d_recv.at[HALF + d], (row + d, rep),
            ).wait_recv()
    for q in range(quart):
        result = section_sum(HALF, q)
        for d in offsets:
            result = result + back_recv[(HALF + d) * quart + q].astype(jnp.float32)
        grad_features_ref[q * blk:(q + 1) * blk] = result.T

    for mask in reversed(masks):
        gather_copy(mask, flip_all(rep, mask)).wait_recv()
    grad_weight_ref[...] = gw_all[...] * (rows * blocks * blk) ** (-0.5)

    for d in offsets:
        @pl.when(inside(d))
        def _():
            feature_copy(d).wait_send()
            grad_copy(d).wait_send()
    for mask in masks:
        part_copy(mask).wait_send()
        back_copy(mask, rep).wait_send()
        scatter_copy(mask).wait_send()
        gather_copy(mask, rep).wait_send()
    for k in range(len(bits)):
        row_copy(k).wait_send()


def make_plan(block_cols, quart):
    blocks, slots = block_cols.shape
    pairs = blocks * slots
    spots = SECTIONS * quart
    first = (lax.axis_index("row") - HALF) * blocks + lax.axis_index("rep") * quart
    moved = block_cols.reshape(pairs) - first
    slot = (moved // blocks) * quart + moved % blocks
    order = jnp.arange(pairs, dtype=jnp.int32)
    key = slot * pairs + order
    place = jnp.sum((key[None, :] < key[:, None]).astype(jnp.int32), axis=1)
    hot = (place[:, None] == order[None, :]).astype(jnp.int32)
    pair = jnp.sum(hot * order[:, None], axis=0)
    sorted_slot = jnp.sum(hot * slot[:, None], axis=0)
    same = (sorted_slot[1:] == sorted_slot[:-1]).astype(jnp.int32)
    keep = jnp.concatenate([jnp.zeros((1,), jnp.int32), same])
    spot = jnp.arange(spots, dtype=jnp.int32)
    ends = jnp.sum((slot[:, None] <= spot[None, :]).astype(jnp.int32), axis=0)
    some = jnp.sum((slot[:, None] == spot[None, :]).astype(jnp.int32), axis=0)
    last = jnp.maximum(ends - 1, 0)
    return jnp.concatenate([slot, pair, pair // slots, keep, last, some])


def on_device(rows, reps, features, block_cols, block_vals, weight, cotangent):
    group_rows, hidden = features.shape
    blocks, _, slots = block_cols.shape
    blk = block_vals.shape[-1]
    quart = blocks // reps
    pairs = blocks * slots
    own_rows = quart * blk
    steps = rows.bit_length() - 1
    share = hidden // reps
    plan = make_plan(block_cols[:, 0, :], quart)
    dma = pltpu.SemaphoreType.DMA
    bf16, f32 = jnp.bfloat16, jnp.float32
    vmem = pl.BlockSpec(memory_space=pltpu.VMEM)
    hbm = pl.BlockSpec(memory_space=pl.ANY)
    return pl.pallas_call(
        functools.partial(layer_kernel, (rows, reps, quart, slots, blk, blocks)),
        out_shape=(
            jax.ShapeDtypeStruct((own_rows, hidden), bf16),
            jax.ShapeDtypeStruct((hidden, hidden), f32),
            jax.ShapeDtypeStruct((own_rows, hidden), f32),
        ),
        in_specs=[pl.BlockSpec(memory_space=pltpu.SMEM), hbm, hbm, vmem, vmem],
        out_specs=(vmem, vmem, vmem),
        scratch_shapes=[
            pltpu.VMEM((pairs, blk, blk), bf16),
            pltpu.VMEM((SECTIONS * quart, blk, hidden), bf16),
            pltpu.VMEM((reps - 1, own_rows, hidden), bf16),
            pltpu.VMEM((reps - 1, own_rows, hidden), bf16),
            pltpu.VMEM((blocks, hidden, blk), bf16),
            pltpu.VMEM((pairs, hidden, blk), f32),
            pltpu.VMEM((SECTIONS * quart, hidden, blk), bf16),
            pltpu.VMEM((SECTIONS * quart, hidden, blk), bf16),
            pltpu.VMEM((hidden, hidden), f32),
            pltpu.VMEM((reps - 1, share, hidden), f32),
            pltpu.VMEM((steps, share, hidden), f32),
            pltpu.VMEM((steps, share, hidden), f32),
            pltpu.VMEM((hidden, hidden), f32),
            dma((2,)),
            dma((SECTIONS,)), dma((SECTIONS,)),
            dma((reps - 1,)), dma((reps - 1,)),
            dma((reps - 1,)), dma((reps - 1,)),
            dma((SECTIONS,)), dma((SECTIONS,)),
            dma((reps - 1,)), dma((reps - 1,)),
            dma((steps,)), dma((steps,)),
            dma((reps - 1,)), dma((reps - 1,)),
        ],
        compiler_params=pltpu.CompilerParams(
            collective_id=0, has_side_effects=True, vmem_limit_bytes=48 * 1024 * 1024
        ),
        cost_estimate=pl.CostEstimate(
            flops=4 * pairs * blk * blk * hidden, bytes_accessed=pairs * blk * blk * 2,
            transcendentals=own_rows * hidden,
        ),
    )(
        plan,
        features.reshape(blocks, blk, hidden),
        block_vals.reshape(pairs, blk, blk),
        weight,
        cotangent,
    )


def solution(mesh):
    return jax.shard_map(
        functools.partial(on_device, mesh.shape["row"], mesh.shape["rep"]),
        mesh=mesh,
        in_specs=(
            P("row", None),
            P("row", "rep", None),
            P("row", "rep", None, None, None),
            P(),
            P(("row", "rep"), None),
        ),
        out_specs=(P(("row", "rep"), None), P(), P(("row", "rep"), None)),
        check_vma=False,
    )
```

time: 252 us -> 66.7 us (0.26)
  the two profiles are of different devices: /device:TPU:10 before, /device:TPU:0 now
where the time goes in v1:
time: 66.7 us; the launch traced here: 66.4 us
  Pallas kernels  57.6 us (86%)
  local copies, waits for them, and re-layouts  6.96 us (10%)
  other arithmetic  1.22 us (2%)
  between operations  0.67 us (1%)
    pallas_call x1, Pallas kernels, on_device(): pl.pallas_call(functools.partial(layer_kernel, (rows, reps, quart, slots,...  57.6 us
    unnamed x11, local copies, waits for them, and re-layouts  6.8 us

profile of v1, /device:TPU:0, one launch (start us, length us, event | category | flops | bytes accessed | tf_op | source)
XLA Modules:
  0.0 66.4 jit_solution(2480930467639394460)
XLA Ops:
  0.6 0.7 %subtract_reduce_fusion = s32[8,12]{1,0:T(8,128)S(1)} fusion(s32[8,1,12]{2,1,0:T(1,128)} %param.6, s32[]{:T(128)S(6)} %add.60), kind=kLoop, calls=%fused_computation.8 | loop fusion | flops 96 | bytes 772 | tf_op jit(solution)/shard_map/sub | solution.py:294
  1.3 0.1 sub.39
  1.4 0.2 convert_reduce_fusion
  1.6 0.1 select_reduce_fusion
  1.7 0.1 compare_convert_fusion
  1.8 0.1 convert_reduce_fusion.1
  2.0 0.1 concatenate.3.plan_ref
  2.0 0.0 copy-start
  2.0 1.9 %copy-done = bf16[8,1,12,128,128]{4,3,2,1,0:T(8,128)(2,1)S(1)} copy-done((bf16[8,1,12,128,128]{4,3,2,1,0:T(8,128)(2,1)S(1)}, bf16[8,1,12,128,128]{4,3,2,1,0:T(8,128)(2,1)}, u32[]{:S(2)}) %copy-start) | copy-done | bytes 3145752
  3.9 0.0 copy-start.1
  3.9 1.0 %copy-done.1 = bf16[1024,256]{1,0:T(8,128)(2,1)S(1)} copy-done((bf16[1024,256]{1,0:T(8,128)(2,1)S(1)}, bf16[1024,256]{1,0:T(8,128)(2,1)}, u32[]{:S(2)}) %copy-start.1) | copy-done | bytes 524312
  5.0 0.0 copy-start.2
  5.0 0.9 %copy-done.2 = bf16[256,256]{1,0:T(8,128)(2,1)S(1)} copy-done((bf16[256,256]{1,0:T(8,128)(2,1)S(1)}, bf16[256,256]{1,0:T(8,128)(2,1)}, u32[]{:S(2)}) %copy-start.2) | copy-done | bytes 131096
  5.9 0.0 copy-start.3
  5.9 0.9 %copy-done.3 = bf16[256,256]{1,0:T(8,128)(2,1)S(1)} copy-done((bf16[256,256]{1,0:T(8,128)(2,1)S(1)}, bf16[256,256]{1,0:T(8,128)(2,1)}, u32[]{:S(2)}) %copy-start.3) | copy-done | bytes 131096
  6.8 57.6 %shard_map.76 = (bf16[256,256]{1,0:T(8,128)(2,1)S(1)}, f32[256,256]{1,0:T(8,128)S(1)}, f32[256,256]{1,0:T(8,128)S(1)}) custom-call(s32[412]{0:T(512)S(1)} %concatenate.3.plan_ref, bf16[8,128,256]{2,1,0:T(8,128)(2,1)S(1)} %bitcast.3, bf16[96,128,128]{2,1,0:T(8,128)(2,1)S(1)} %bitcast.2, bf16[256,256]{1,0:T(8,128)(2,1)S(1)} %copy-done.2, ...), custom_call_target="tpu_custom_call" | custom-call | flops 1610612736 | bytes 3145728 | tf_op jit(solution)/shard_map/pallas_call | solution.py:325
  64.4 0.7 copy.11
  65.0 0.7 %copy.12 = f32[256,256]{1,0:T(8,128)} copy(f32[256,256]{1,0:T(8,128)S(1)} %get-tuple-element.13) | data formatting | bytes 524288
  65.7 0.7 %copy.13 = f32[256,256]{1,0:T(8,128)} copy(f32[256,256]{1,0:T(8,128)S(1)} %get-tuple-element.14) | data formatting | bytes 524288
  (3 shorter events, 0.0 us)
Async XLA Ops:
  2.0 1.9 %copy-start = (bf16[8,1,12,128,128]{4,3,2,1,0:T(8,128)(2,1)S(1)}, bf16[8,1,12,128,128]{4,3,2,1,0:T(8,128)(2,1)}, u32[]{:S(2)}) copy-start(bf16[8,1,12,128,128]{4,3,2,1,0:T(8,128)(2,1)} %param.7) | copy-start | bytes 9437188
  3.9 1.0 %copy-start.1 = (bf16[1024,256]{1,0:T(8,128)(2,1)S(1)}, bf16[1024,256]{1,0:T(8,128)(2,1)}, u32[]{:S(2)}) copy-start(bf16[1024,256]{1,0:T(8,128)(2,1)} %param.5) | copy-start | bytes 1572868
  5.0 0.9 %copy-start.2 = (bf16[256,256]{1,0:T(8,128)(2,1)S(1)}, bf16[256,256]{1,0:T(8,128)(2,1)}, u32[]{:S(2)}) copy-start(bf16[256,256]{1,0:T(8,128)(2,1)} %weight_ref.1) | copy-start | bytes 393220
  5.9 0.9 %copy-start.3 = (bf16[256,256]{1,0:T(8,128)(2,1)S(1)}, bf16[256,256]{1,0:T(8,128)(2,1)}, u32[]{:S(2)}) copy-start(bf16[256,256]{1,0:T(8,128)(2,1)} %cotangent_ref.1) | copy-start | bytes 393220
